TPU v7x, 128 devices: a whole 4x4x4 slice. The times are simulated.
128 devices in a mesh: row: 16 (over y, x), col: 4 (over z), depth: 2 (over core).
Axes of the slice: x: 4, y: 4, z: 4, core: 2. Of those that a mesh axis runs over, the one named last changes fastest.
Arguments:
- upper: float32 [8192, 8192], P('row', 'col'), may hold values from -0.25 to 0.25
- pattern: int32 [64, 64], replicated, may hold values from 0 to 1, as said below
Outputs:
- purified: float32 [8192, 8192], P('row', 'col')
Inputs may be any that keep to these rules, and one draw needn't show every extreme that they name: `pattern`: block pairs near the diagonal are present; a few far pairs are present too.
All inputs are finite; a program needn't handle non-finite values.
Results may differ from a plain program's by a relative error of at most 0.00007.
Values sent between devices are 32-bit elements; how exact they have to be, the bound alone decides.
No kernel may reach another device: no remote copies, remote signals or barrier semaphores. Data moves between devices by JAX's collectives and lax.ppermute only.
A program may use at most 128 MiB of HBM per device.

v0:
```python
import jax
import jax.numpy as jnp
from jax import lax
from jax.experimental import pallas as pl
from jax.experimental.pallas import tpu as pltpu
from jax.sharding import PartitionSpec as P

BS = 128
NB = 64
ROWS = 4
COLS = 16
NROW = 16
NCOL = 4
STRIPS = 16
PER = 44
PARTS = 4
PART = PER // PARTS
ITEMS = 256
CAP = 8 * PER
SRC = 3
HALF = 2
MR = HALF * BS
UNROLL = 12
VMEM = 62 * 1024 * 1024
ALL = ("row", "col", "depth")


def prefix(ones):
    ids = jnp.arange(NB, dtype=jnp.int32)
    before = (ids[:, None] < ids[None, :]).astype(jnp.float32)
    return jnp.dot(ones.astype(jnp.float32), before, preferred_element_type=jnp.float32).astype(jnp.int32)


def layout(pattern):
    ids = jnp.arange(NB, dtype=jnp.int32)
    stored = jnp.where(ids[:, None] < ids[None, :], pattern, 0) + (ids[:, None] == ids[None, :])
    stored = (stored != 0).astype(jnp.int32)
    local = stored.reshape(NROW, ROWS, NCOL, COLS).transpose(0, 2, 1, 3).reshape(NB, NB)
    rank = prefix(local)
    count = jnp.sum(local, axis=1)
    first = prefix(count[None, :])[0]
    last = first + count
    slot = (first[:, None] + rank).reshape(NROW, NCOL, ROWS, COLS).transpose(0, 2, 1, 3).reshape(NB, NB)
    fits = jnp.all(count <= 8 * SRC) & (last[NB - 1] <= CAP)
    return stored, slot, first, last, fits


def pack_kernel(here_ref, pattern_ref, pattern_vec, upper_ref, out_ref, list_ref, sem):
    row, col, depth = here_ref[0], here_ref[1], here_ref[2]
    i = lax.broadcasted_iota(jnp.int32, (NB, NB), 0)
    j = lax.broadcasted_iota(jnp.int32, (NB, NB), 1)
    stored = (i == j) | ((i < j) & (pattern_vec[...] != 0))
    earlier = (i // ROWS) * NCOL + j // COLS < row * NCOL + col
    first = jnp.sum(jnp.where(stored & earlier, 1.0, 0.0)).astype(jnp.int32)

    def copy(at):
        code = list_ref[at]
        a, b, n = code & 3, (code >> 2) & 15, code >> 6
        return pltpu.make_async_copy(
            upper_ref.at[pl.ds(a * STRIPS, STRIPS), :, pl.ds(pl.multiple_of(b * BS, BS), BS)],
            out_ref.at[:, ((first + n) >> 1) & 3, n >> 3],
            sem.at[at],
        )

    def find(a, state):
        def one(b, state):
            n, at = state
            i, j = row * ROWS + a, col * COLS + b
            there = (i == j) | ((i < j) & (pattern_ref[i, j] != 0))
            ours = there & (((first + n) & 1) == depth) & (n < 8 * SRC)

            @pl.when(ours)
            def _():
                list_ref[at] = a + 4 * b + 64 * n
                copy(at).start()

            return n + there.astype(jnp.int32), at + ours.astype(jnp.int32)

        return lax.fori_loop(0, COLS, one, state, unroll=4)

    _, found = lax.fori_loop(0, ROWS, find, (jnp.int32(0), jnp.int32(0)))

    def finish(at, _):
        copy(at).wait()
        code = list_ref[at]
        a, b, n = code & 3, (code >> 2) & 15, code >> 6

        @pl.when(row * ROWS + a == col * COLS + b)
        def _():
            z = ((first + n) >> 1) & 3
            x = out_ref[:, z, n >> 3].reshape(BS, BS)
            out_ref[:, z, n >> 3] = (0.5 * (x + x.T)).reshape(STRIPS, 8, BS)

        return 0

    lax.fori_loop(0, found, finish, 0)


def select_kernel(index_ref, got_ref, out_ref):
    for u in range(PER):
        out_ref[u] = got_ref[index_ref[u]]


def split(x):
    high = x.astype(jnp.bfloat16)
    return high, (x - high.astype(jnp.float32)).astype(jnp.bfloat16)


def main_kernel(sd_ref, st_ref, pd_ref, pt_ref, item_ref, limit_ref, row_ref, rn_ref, where_ref,
                blocks_hbm, out_ref, blocks_ref, a_ref, s_ref, sum_ref, cube_ref, sem, row_sem):
    first_col = where_ref[0]

    def row_load(h, p, n):
        slot = (row_ref[h, p] >> 7) & 511
        return pltpu.make_async_copy(
            blocks_hbm.at[:, slot & 7, slot >> 3], sum_ref.at[n >> 1, pl.ds((n & 1) * STRIPS, STRIPS)], row_sem.at[n]
        )

    for h in range(HALF):
        def start(p, _, h=h):
            row_load(h, p, h * NB + p).start()
            return 0

        lax.fori_loop(0, rn_ref[h], start, 0)
    loads = [
        pltpu.make_async_copy(
            blocks_hbm.at[:, :, pl.ds(i * PART, PART)], blocks_ref.at[:, :, pl.ds(i * PART, PART)], sem.at[i]
        )
        for i in range(PARTS)
    ]
    for load in loads:
        load.start()
    a_ref[...] = jnp.zeros_like(a_ref)
    cube_ref[...] = jnp.zeros_like(cube_ref)
    s_ref[NB] = jnp.zeros((2 * MR, BS), jnp.bfloat16)

    def block(slot):
        return blocks_ref[:, slot & 7, slot >> 3].reshape(BS, BS)

    for h in range(HALF):
        def fill(p, _, h=h):
            code = row_ref[h, p]
            m = code & 127
            n = h * NB + p
            row_load(h, p, n).wait()
            x = sum_ref[n >> 1, pl.ds((n & 1) * STRIPS, STRIPS)].reshape(BS, BS)

            def put(x):
                high, low = split(x)
                a_ref[m, h * BS:(h + 1) * BS] = high
                a_ref[m, MR + h * BS:MR + (h + 1) * BS] = low

            @pl.when(code < 65536)
            def _():
                put(x)

            @pl.when(code >= 65536)
            def _():
                put(x.T)

            return 0

        lax.fori_loop(0, rn_ref[h], fill, 0)
    sum_ref[...] = jnp.zeros_like(sum_ref)

    def product(left_ref, list_ref, mirrored, k, p):
        c0, c1 = list_ref[k, p], list_ref[k, p + 1]
        left = jnp.concatenate([left_ref[c0 & 127], left_ref[c1 & 127]], axis=1)
        h0, l0 = split(block(c0 >> 7))
        h1, l1 = split(block(c1 >> 7))
        if mirrored:
            right = jnp.concatenate([jnp.concatenate([h0, h1], axis=1), jnp.concatenate([l0, l1], axis=1)], axis=0)
            z = lax.dot_general(left, right, (((1,), (1,)), ((), ())), preferred_element_type=jnp.float32)
        else:
            right = jnp.concatenate([jnp.concatenate([h0, l0], axis=1), jnp.concatenate([h1, l1], axis=1)], axis=0)
            z = jnp.dot(left, right, preferred_element_type=jnp.float32)
        z = z[:MR] + z[MR:]
        return z[:, :BS] + z[:, BS:]

    def work(left_ref, list_ref, mirrored, into_ref, at, begin, end):
        def several(i, _):
            items = [item_ref[at, UNROLL * i + e] for e in range(UNROLL)]
            done = [product(left_ref, list_ref, mirrored, item >> 6, item & 63) for item in items]
            for item, z in zip(items, done):
                into_ref[item >> 6] += z.reshape(MR // 8, 8, BS)
            return 0

        lax.fori_loop(begin, end, several, 0)

    begin = 0
    for i, load in enumerate(loads):
        load.wait()
        end = limit_ref[4 + i]
        work(a_ref, st_ref, True, sum_ref, 1, begin, end)
        begin = end
    work(a_ref, sd_ref, False, sum_ref, 0, 0, limit_ref[0])

    def halves(k, _):
        high, low = split(sum_ref[k].reshape(MR, BS))
        s_ref[k, :MR] = high
        s_ref[k, MR:] = low
        return 0

    lax.fori_loop(0, NB, halves, 0, unroll=2)
    work(s_ref, pd_ref, False, cube_ref, 2, 0, limit_ref[2])
    work(s_ref, pt_ref, True, cube_ref, 3, 0, limit_ref[3])
    for j in range(COLS):
        out_ref[:, j * BS:(j + 1) * BS] = (3.0 * sum_ref[first_col + j] - 2.0 * cube_ref[j]).reshape(MR, BS)


def compact(chosen, codes, pad):
    ids = jnp.arange(NB, dtype=jnp.int32)
    at = jnp.where(chosen, prefix(chosen), -1)
    hit = at[:, :, None] == ids[None, None, :]
    table = pad + jnp.sum(jnp.where(hit, (codes - pad)[:, :, None], 0), axis=1)
    return jnp.pad(table, ((0, 1), (0, 0)), constant_values=pad)


def count(chosen):
    return jnp.sum(chosen.astype(jnp.int32), axis=1)


def flat_items(chosen, mirrored_table):
    columns = jnp.array([[x.shape[0]] for x in chosen], jnp.int32)
    pairs = jnp.stack([jnp.pad((count(x) + 1) >> 1, (0, NB - x.shape[0])) for x in chosen])
    begin = prefix(pairs)
    end = begin + pairs
    total = end[:, NB - 1:]
    p = jnp.arange(ITEMS, dtype=jnp.int32)
    before = end[:, None, :] <= p[None, :, None]
    column = jnp.sum(before.astype(jnp.int32), axis=2)
    offset = p[None, :] - jnp.max(jnp.where(before, end[:, None, :], 0), axis=2)
    items = jnp.where(p[None, :] < total, column * NB + 2 * offset, columns * NB)
    place = jnp.max(mirrored_table[:NB].reshape(NB, NB // 2, 2), axis=2) >> 10
    i = jnp.arange(NB // 2, dtype=jnp.int32)[None, :]
    at = jnp.where(i < pairs[1][:, None], begin[1][:, None] + i, ITEMS)
    ends = [
        jnp.minimum(jnp.min(jnp.where(place >= c * PART, at, ITEMS)), total[1, 0]) // UNROLL for c in range(1, PARTS)
    ]
    rounds = (total[:, 0] + UNROLL - 1) // UNROLL
    return items, jnp.concatenate([rounds, jnp.stack(ends), rounds[1:2]])


SMEM = pl.BlockSpec(memory_space=pltpu.SMEM)
INVMEM = pl.BlockSpec(memory_space=pltpu.VMEM)
ANY = pl.BlockSpec(memory_space=pl.ANY)


def gather(upper, pattern, first, last):
    ids = jnp.arange(NB, dtype=jnp.int32)
    row, col, depth = lax.axis_index("row"), lax.axis_index("col"), lax.axis_index("depth")
    packed = pl.pallas_call(
        pack_kernel,
        out_shape=jax.ShapeDtypeStruct((STRIPS, NCOL, SRC, 8, BS), jnp.float32),
        in_specs=[SMEM, SMEM, INVMEM, ANY],
        out_specs=INVMEM,
        scratch_shapes=[pltpu.SMEM((8 * SRC,), jnp.int32), pltpu.SemaphoreType.DMA((8 * SRC,))],
        compiler_params=pltpu.CompilerParams(vmem_limit_bytes=16 * 1024 * 1024),
    )(jnp.stack([row, col, depth]).astype(jnp.int32), pattern, pattern, upper.reshape(ROWS * STRIPS, 8, COLS * BS))
    got = lax.all_to_all(packed.reshape(NB, SRC * 8, BS), ("row", "col"), 0, 0, tiled=True)
    g = 8 * jnp.arange(PER, dtype=jnp.int32) + 2 * col + depth
    source = jnp.minimum(jnp.sum((last[None, :] <= g[:, None]).astype(jnp.int32), axis=1), NB - 1)
    source_first = jnp.sum(jnp.where(source[:, None] == ids[None, :], first[None, :], 0), axis=1)
    pick = source * SRC + jnp.clip((g - source_first) >> 3, 0, SRC - 1)
    share = pl.pallas_call(
        select_kernel,
        out_shape=jax.ShapeDtypeStruct((PER, 8, BS), jnp.float32),
        in_specs=[SMEM, INVMEM],
        out_specs=INVMEM,
        compiler_params=pltpu.CompilerParams(vmem_limit_bytes=16 * 1024 * 1024),
    )(pick, got.reshape(NB * SRC, 8, BS))
    return lax.all_gather(share, ALL, axis=0).reshape(STRIPS, 8, PER, 8, BS)


def work_lists(stored, slot):
    ids = jnp.arange(NB, dtype=jnp.int32)
    row, col, depth = lax.axis_index("row"), lax.axis_index("col"), lax.axis_index("depth")
    below = ids[:, None] > ids[None, :]
    both = jnp.where(below, stored.T, stored) != 0
    slots = jnp.where(below, slot.T, slot)
    codes = ids[None, :] + BS * slots
    my_row = row * ROWS + depth * HALF
    near = jnp.any(lax.dynamic_slice_in_dim(both, my_row, HALF, 0), axis=0)
    direct = both & (ids[None, :] <= ids[:, None])
    mirrored = both & (ids[None, :] > ids[:, None])
    sd, st = direct & near[None, :], mirrored & near[None, :]
    col_direct = lax.dynamic_slice_in_dim(direct, col * COLS, COLS, 0)
    col_mirrored = lax.dynamic_slice_in_dim(mirrored, col * COLS, COLS, 0)
    col_codes = lax.dynamic_slice_in_dim(codes, col * COLS, COLS, 0)
    row_both = lax.dynamic_slice_in_dim(both, my_row, HALF, 0)
    row_codes = lax.dynamic_slice_in_dim(codes + 65536 * below, my_row, HALF, 0)
    st_table = compact(st, codes, NB)
    items, limits = flat_items((sd, st, col_direct, col_mirrored), st_table)
    return (
        compact(sd, codes, NB), st_table, compact(col_direct, col_codes, NB), compact(col_mirrored, col_codes, NB),
        items, limits, compact(row_both, row_codes, NB), count(row_both), (col * COLS)[None].astype(jnp.int32),
    )


def multiply(upper, pattern, blocks, *lists):
    return pl.pallas_call(
        main_kernel,
        out_shape=jax.ShapeDtypeStruct((MR, COLS * BS), jnp.float32),
        in_specs=[SMEM] * 9 + [ANY],
        out_specs=INVMEM,
        scratch_shapes=[
            pltpu.VMEM((STRIPS, 8, PER, 8, BS), jnp.float32),
            pltpu.VMEM((NB + 1, 2 * MR, BS), jnp.bfloat16),
            pltpu.VMEM((NB + 1, 2 * MR, BS), jnp.bfloat16),
            pltpu.VMEM((NB + 1, MR // 8, 8, BS), jnp.float32),
            pltpu.VMEM((COLS + 1, MR // 8, 8, BS), jnp.float32),
            pltpu.SemaphoreType.DMA((PARTS,)),
            pltpu.SemaphoreType.DMA((HALF * NB,)),
        ],
        compiler_params=pltpu.CompilerParams(vmem_limit_bytes=VMEM),
    )(*lists, blocks)


def join_kernel(depth_ref, mine_ref, other_ref, out_ref, held_ref, in_sem, out_sem):
    depth = depth_ref[0]
    rows = MR // 4
    loads, stores = [], []
    for i in range(8):
        part_ref, half = ((mine_ref, depth), (other_ref, 1 - depth))[i % 2]
        at = i // 2 * rows
        to = pl.multiple_of(half * MR + at, rows)
        loads.append(pltpu.make_async_copy(part_ref.at[pl.ds(at, rows)], held_ref.at[i], in_sem.at[i]))
        stores.append(pltpu.make_async_copy(held_ref.at[i], out_ref.at[pl.ds(to, rows)], out_sem.at[i]))
    for load in loads:
        load.start()
    for load, store in zip(loads, stores):
        load.wait()
        store.start()
    for store in stores:
        store.wait()


def dense(upper, pattern):
    rows_tile, cols_tile = upper.shape
    nrow = lax.axis_size("row")
    ncol = lax.axis_size("col")
    ndep = lax.axis_size("depth")
    row_blocks = rows_tile // BS
    col_blocks = cols_tile // BS
    spread = upper.reshape(row_blocks, ncol, BS // ncol, col_blocks, nrow, BS // nrow)
    spread = spread.transpose(4, 1, 0, 2, 3, 5).reshape(
        nrow * ncol, row_blocks, BS // ncol, col_blocks, BS // nrow
    )
    spread = lax.all_to_all(spread, ("row", "col"), split_axis=0, concat_axis=0, tiled=True)
    spread = spread.reshape(nrow, ncol, row_blocks, BS // ncol, col_blocks, BS // nrow)
    spread = spread.transpose(0, 2, 3, 1, 4, 5).reshape(
        ncol, col_blocks, BS // ncol, nrow, row_blocks, BS // nrow
    )
    spread = spread.transpose(3, 0, 4, 5, 1, 2).reshape(
        nrow * ncol, row_blocks, BS // nrow, col_blocks, BS // ncol
    )
    spread = lax.all_to_all(spread, ("row", "col"), split_axis=0, concat_axis=0, tiled=True)
    spread = spread.reshape(nrow, ncol, row_blocks, BS // nrow, col_blocks, BS // ncol)
    mirror = spread.transpose(2, 0, 3, 4, 1, 5).reshape(row_blocks, BS, col_blocks, BS)
    row_index = lax.axis_index("row")
    col_index = lax.axis_index("col")
    row_first = row_index * row_blocks
    col_first = col_index * col_blocks
    global_rows = row_first + jnp.arange(row_blocks, dtype=jnp.int32)
    global_cols = col_first + jnp.arange(col_blocks, dtype=jnp.int32)
    above = global_rows[:, None] < global_cols[None, :]
    below = global_rows[:, None] > global_cols[None, :]
    upper_pat = lax.dynamic_slice(pattern, (row_first, col_first), (row_blocks, col_blocks))
    lower_pat = lax.dynamic_slice(pattern, (col_first, row_first), (col_blocks, row_blocks)).T
    keep = jnp.where(above, upper_pat, jnp.where(below, lower_pat, 1)).astype(jnp.float32)
    own = upper.reshape(row_blocks, BS, col_blocks, BS)
    blended = jnp.where(
        above[:, None, :, None],
        own,
        jnp.where(below[:, None, :, None], mirror, 0.5 * (own + mirror)),
    )
    density = (blended * keep[:, None, :, None]).reshape(rows_tile, cols_tile)
    layer = lax.axis_index("depth")

    def layer_columns(tile):
        split = tile.reshape(rows_tile, col_blocks // ndep, ndep, BS)
        return lax.dynamic_slice_in_dim(split, layer, 1, 2).reshape(
            rows_tile, col_blocks // ndep * BS
        )

    split_rows = density.reshape(row_blocks // ndep, ndep, BS, cols_tile)
    layer_rows = lax.dynamic_slice_in_dim(split_rows, layer, 1, 1).reshape(
        row_blocks // ndep * BS, cols_tile
    )
    panel = lax.all_gather(layer_rows, "row", axis=0, tiled=True)

    def accumulate(piece):
        return jnp.dot(
            piece, panel, precision=lax.Precision.HIGHEST, preferred_element_type=jnp.float32
        )

    square_part = accumulate(lax.all_gather(layer_columns(density), "col", axis=1, tiled=True))
    square = lax.psum(square_part, "depth")
    cube_part = accumulate(lax.all_gather(layer_columns(square), "col", axis=1, tiled=True))
    cube = lax.psum(cube_part, "depth")
    return 3.0 * square - 2.0 * cube


def dense_half(upper, pattern, *rest):
    return lax.dynamic_slice_in_dim(dense(upper, pattern), lax.axis_index("depth") * MR, MR, 0)


def local(upper, pattern):
    stored, slot, first, last, fits = layout(pattern)
    blocks = gather(upper, pattern, first, last)
    lists = lax.optimization_barrier(work_lists(stored, slot))
    mine = lax.cond(fits, multiply, dense_half, upper, pattern, blocks, *lists)
    other = lax.ppermute(mine, "depth", [(0, 1), (1, 0)])
    return pl.pallas_call(
        join_kernel,
        out_shape=jax.ShapeDtypeStruct(upper.shape, jnp.float32),
        in_specs=[SMEM, ANY, ANY],
        out_specs=ANY,
        scratch_shapes=[
            pltpu.VMEM((8, MR // 4, COLS * BS), jnp.float32),
            pltpu.SemaphoreType.DMA((8,)),
            pltpu.SemaphoreType.DMA((8,)),
        ],
        compiler_params=pltpu.CompilerParams(vmem_limit_bytes=16 * 1024 * 1024),
    )(lax.axis_index("depth")[None].astype(jnp.int32), mine, other)


def solution(mesh):
    placed = (P("row", "col"), P())
    return jax.shard_map(
        local, mesh=mesh, in_specs=placed, out_specs=P("row", "col"), check_vma=False
    )
```

profile of v0, /device:TPU:1, one launch (start us, length us, event | category | flops | bytes accessed | tf_op | source)
XLA Modules:
  0.0 169.4 jit_solution(15820921305334351869)
XLA Ops:
  6.6 4.7 %shard_map.37 = f32[16,4,3,8,128]{4,3,2,1,0:T(8,128)} custom-call(s32[3]{0:T(128)S(1)} %pad_add_fusion.1.here_ref, s32[64,64]{1,0:T(8,128)} %pattern_vec.1, s32[64,64]{1,0:T(8,128)} %pattern_vec.1, f32[64,8,2048]{2,1,0:T(8,128)} %bitcast.98), custom_call_target="tpu_custom_call" | custom-call | tf_op jit(solution)/shard_map/pallas_call | solution.py:252
  11.3 12.0 %all-to-all-start.2 = ((f32[64,24,128]{2,1,0:T(8,128)}), f32[64,24,128]{2,1,0:T(8,128)S(1)}, u32[]{:S(2)}, u32[]{:S(2)}) async-start(f32[64,24,128]{2,1,0:T(8,128)} %bitcast.24), calls=%async_computation.2 | async-start | bytes 1572864 | tf_op jit(solution)/shard_map/all_to_all | solution.py:260
  23.6 1.2 bitcast_reduce_fusion
  25.1 0.2 convert_reduce_fusion.3
  25.2 0.2 select_reduce_fusion.6
  25.4 12.3 %all-to-all-done.2 = f32[64,24,128]{2,1,0:T(8,128)S(1)} async-done(((f32[64,24,128]{2,1,0:T(8,128)}), f32[64,24,128]{2,1,0:T(8,128)S(1)}, u32[]{:S(2)}, u32[]{:S(2)}) %all-to-all-start.2) | async-done | bytes 786464 | tf_op jit(solution)/shard_map/all_to_all | solution.py:260
  37.8 1.2 shard_map.38
  39.1 0.5 slice.19
  40.2 0.6 slice.22
  41.0 0.2 reshape.214
  41.5 0.1 fusion.3
  41.8 2.3 %select_reduce_fusion = (s32[64,64]{1,0:T(8,128)S(1)}, s32[64,64]{1,0:T(8,128)S(1)}) fusion(s32[64,64]{1,0:T(8,128)S(1)} %fusion.3, s32[64,64]{1,0:T(8,128)S(1)} %get-tuple-element.129, s32[64,64]{1,0:T(8,128)S(1)} %fusion.5), kind=kLoop, calls=%fused_computation.21 | loop fusion | flops 1564672 | bytes 81920 | tf_op jit(solution)/shard_map/reduce_sum | solution.py:215
  44.2 0.7 select_reduce_fusion.7
  48.7 0.2 slice_reduce_fusion
  48.9 0.6 slice.23
  50.0 0.6 compare_reduce_fusion
  51.9 0.6 select_reduce_fusion.2
  52.6 0.7 concatenate.3
  53.3 0.1 convert_reduce_fusion
  53.5 73.6 %all-gather.12.cloned.1.call-done = f32[5632,8,128]{2,1,0:T(8,128)} async-done(((f32[44,8,128]{2,1,0:T(8,128)}), f32[5632,8,128]{2,1,0:T(8,128)}) %all-gather.12.cloned.1.call-update) | async-done | bytes 23068688 | tf_op jit(solution)/shard_map/all_gather | solution.py:272
  127.1 27.8 %conditional.1 = (f32[256,2048]{1,0:T(8,128)}) conditional(s32[]{:T(128)} %convert_element_type.91, (f32[512,2048]{1,0:T(8,128)}, s32[64,64]{1,0:T(8,128)S(1)}) %tuple.59, (f32[128,44,8,128]{3,2,1,0:T(8,128)}, s32[65,64]{1,0:T(8,128)S(1)}, s32[65,64]{1,0:T(8,128)S(1)}, s32[17,64]{1,0:T(8,128)S(1)}, s32[17,64]{1,0:T(8,128)S(1)}, ...), branch_computations={%region_21.24_spmd, %region_24.25_spmd} | conditional | flops 103088128000 | bytes 503794816 | solution.py:412
  127.1 27.8 %branch_1_fun.1 = f32[256,2048]{1,0:T(8,128)} custom-call(s32[65,64]{1,0:T(8,128)S(1)} %get-tuple-element.35.sd_ref, s32[65,64]{1,0:T(8,128)S(1)} %get-tuple-element.36.st_ref, s32[17,64]{1,0:T(8,128)S(1)} %get-tuple-element.37.pd_ref, s32[17,64]{1,0:T(8,128)S(1)} %get-tuple-element.38.pt_ref, s32[4,256]{1,0:T(4,128)S(1)} %get-tuple-element.39.item_ref, ...), custom_call_target="tpu_custom_call" | custom-call | tf_op jit(solution)/shard_map/cond/branch_1_fun/pallas_call | solution.py:301
  155.0 4.4 %collective-permute-done.other_ref = f32[256,2048]{1,0:T(8,128)S(1)} collective-permute-done((f32[256,2048]{1,0:T(8,128)}, f32[256,2048]{1,0:T(8,128)S(1)}, u32[]{:S(2)}, u32[]{:S(2)}) %collective-permute-start) | collective-permute-done | bytes 2097184 | tf_op jit(solution)/shard_map/ppermute | solution.py:413
  159.3 3.2 %shard_map.39 = f32[512,2048]{1,0:T(8,128)} custom-call(s32[1]{0:T(128)} %bitcast.16.depth_ref, f32[256,2048]{1,0:T(8,128)} %get-tuple-element.150.mine_ref, f32[256,2048]{1,0:T(8,128)S(1)} %collective-permute-done.other_ref), custom_call_target="tpu_custom_call" | custom-call | tf_op jit(solution)/shard_map/pallas_call | solution.py:414
  (56 shorter events, 2.8 us)
Async XLA Ops:
  6.5 16.8 %copy-start = (s32[64,64]{1,0:T(8,128)S(1)}, s32[64,64]{1,0:T(8,128)}, u32[]{:S(2)}) copy-start(s32[64,64]{1,0:T(8,128)} %pattern_vec.1) | copy-start | bytes 49156
  6.6 46.8 %copy-start.1 = (s32[4]{0:T(128)S(1)}, s32[4]{0:T(128)}, u32[]{:S(2)}) copy-start(s32[4]{0:T(128)} %constant.149) | copy-start | bytes 52
  11.3 26.5 %all-to-all-start.2 = ((f32[64,24,128]{2,1,0:T(8,128)}), f32[64,24,128]{2,1,0:T(8,128)S(1)}, u32[]{:S(2)}, u32[]{:S(2)}) async-start(f32[64,24,128]{2,1,0:T(8,128)} %bitcast.24), calls=%async_computation.2 | async-start | bytes 1572864 | tf_op jit(solution)/shard_map/all_to_all | solution.py:260
  23.3 103.8 %all-gather.12.cloned.1.call-start = ((), (), s32[]{:S(2)}) async-start(), calls=%async_computation.8 | async-start | bytes 23248896 | tf_op jit(solution)/shard_map/all_gather | solution.py:272
  154.9 4.5 %collective-permute-start = (f32[256,2048]{1,0:T(8,128)}, f32[256,2048]{1,0:T(8,128)S(1)}, u32[]{:S(2)}, u32[]{:S(2)}) collective-permute-start(f32[256,2048]{1,0:T(8,128)} %get-tuple-element.150.mine_ref), channel_id=1, source_target_pairs={{0,1},{1,0},{2,3},{3,2},{4,5},{5,4},{6,7},{7,6},{8,9},{9,8},{10,11... | collective-permute-start | bytes 6291464 | tf_op jit(solution)/shard_map/ppermute | solution.py:413
Sparse Core Ops, SparseCore 0:
  39.2 87.8 all-gather.11
where the time goes:
time: 170 us; the launch traced here: 169 us
  waiting for transfers between devices  90.3 us (53%)
  Pallas kernels  36.9 us (22%)
  between operations  18.6 us (11%)
  starting transfers between devices  12.1 us (7%)
  other arithmetic  6.91 us (4%)
  local copies, waits for them, and re-layouts  3.54 us (2%)
    all_gather x1, waiting for transfers between devices, gather(): return lax.all_gather(share, ALL, axis=0).reshape(STRIPS, 8, PER, 8, BS)  73.6 us
    pallas_call x1, Pallas kernels, multiply(): pl.pallas_call(main_kernel, out_shape=jax.ShapeDtypeStruct((MR, COLS * BS...  27.8 us
    all_to_all x1, waiting for transfers between devices, gather(): lax.all_to_all(packed.reshape(NB, SRC * 8, BS), ('row', 'col'), 0, 0, til...  12.3 us
    all_to_all x1, starting transfers between devices, gather(): lax.all_to_all(packed.reshape(NB, SRC * 8, BS), ('row', 'col'), 0, 0, til...  12 us
    pallas_call x1, Pallas kernels, gather(): pl.pallas_call(pack_kernel, out_shape=jax.ShapeDtypeStruct((STRIPS, NCOL,...  4.68 us
    ppermute x1, waiting for transfers between devices, local(): other = lax.ppermute(mine, 'depth', [(0, 1), (1, 0)])  4.36 us
  transfers between devices with their start and end apart: 3, of which 3 were waited for; matrix products, arithmetic and copies ran while one was open for 7% of the time, Pallas kernels for 0%

commit v1 on v0

--- a/solution.py
+++ b/solution.py
@@ -107,8 +107,9 @@
 
 
 def main_kernel(sd_ref, st_ref, pd_ref, pt_ref, item_ref, limit_ref, row_ref, rn_ref, where_ref,
-                blocks_hbm, out_ref, blocks_ref, a_ref, s_ref, sum_ref, cube_ref, sem, row_sem):
+                blocks_hbm, whole_hbm, half_hbm, out_ref, blocks_ref, a_ref, s_ref, sum_ref, cube_ref, sem, row_sem, out_sem):
     first_col = where_ref[0]
+    first_row = pl.multiple_of(where_ref[1] * MR, MR)
 
     def row_load(h, p, n):
         slot = (row_ref[h, p] >> 7) & 511
@@ -204,8 +205,16 @@
     lax.fori_loop(0, NB, halves, 0, unroll=2)
     work(s_ref, pd_ref, False, cube_ref, 2, 0, limit_ref[2])
     work(s_ref, pt_ref, True, cube_ref, 3, 0, limit_ref[3])
+    stores = []
     for j in range(COLS):
         out_ref[:, j * BS:(j + 1) * BS] = (3.0 * sum_ref[first_col + j] - 2.0 * cube_ref[j]).reshape(MR, BS)
+        if j % 4 == 3:
+            columns = pl.ds((j - 3) * BS, 4 * BS)
+            for k, to in enumerate((half_hbm.at[:, columns], whole_hbm.at[pl.ds(first_row, MR), columns])):
+                stores.append(pltpu.make_async_copy(out_ref.at[:, columns], to, out_sem.at[k, j // 4]))
+                stores[-1].start()
+    for store in stores:
+        store.wait()
 
 
 def compact(chosen, codes, pad):
@@ -293,17 +302,21 @@
     items, limits = flat_items((sd, st, col_direct, col_mirrored), st_table)
     return (
         compact(sd, codes, NB), st_table, compact(col_direct, col_codes, NB), compact(col_mirrored, col_codes, NB),
-        items, limits, compact(row_both, row_codes, NB), count(row_both), (col * COLS)[None].astype(jnp.int32),
+        items, limits, compact(row_both, row_codes, NB), count(row_both), jnp.stack([col * COLS, depth]).astype(jnp.int32),
     )
 
 
 def multiply(upper, pattern, blocks, *lists):
-    return pl.pallas_call(
+    whole, half = pl.pallas_call(
         main_kernel,
-        out_shape=jax.ShapeDtypeStruct((MR, COLS * BS), jnp.float32),
+        out_shape=[
+            jax.ShapeDtypeStruct((2 * MR, COLS * BS), jnp.float32),
+            jax.ShapeDtypeStruct((MR, COLS * BS), jnp.float32),
+        ],
         in_specs=[SMEM] * 9 + [ANY],
-        out_specs=INVMEM,
+        out_specs=[ANY, ANY],
         scratch_shapes=[
+            pltpu.VMEM((MR, COLS * BS), jnp.float32),
             pltpu.VMEM((STRIPS, 8, PER, 8, BS), jnp.float32),
             pltpu.VMEM((NB + 1, 2 * MR, BS), jnp.bfloat16),
             pltpu.VMEM((NB + 1, 2 * MR, BS), jnp.bfloat16),
@@ -311,20 +324,20 @@
             pltpu.VMEM((COLS + 1, MR // 8, 8, BS), jnp.float32),
             pltpu.SemaphoreType.DMA((PARTS,)),
             pltpu.SemaphoreType.DMA((HALF * NB,)),
+            pltpu.SemaphoreType.DMA((2, 4)),
         ],
         compiler_params=pltpu.CompilerParams(vmem_limit_bytes=VMEM),
     )(*lists, blocks)
-
-
-def join_kernel(depth_ref, mine_ref, other_ref, out_ref, held_ref, in_sem, out_sem):
-    depth = depth_ref[0]
+    return whole, half
+
+
+def join_kernel(depth_ref, whole_ref, other_ref, out_ref, held_ref, in_sem, out_sem):
+    first_row = (1 - depth_ref[0]) * MR
     rows = MR // 4
     loads, stores = [], []
-    for i in range(8):
-        part_ref, half = ((mine_ref, depth), (other_ref, 1 - depth))[i % 2]
-        at = i // 2 * rows
-        to = pl.multiple_of(half * MR + at, rows)
-        loads.append(pltpu.make_async_copy(part_ref.at[pl.ds(at, rows)], held_ref.at[i], in_sem.at[i]))
+    for i in range(4):
+        to = pl.multiple_of(first_row + i * rows, rows)
+        loads.append(pltpu.make_async_copy(other_ref.at[pl.ds(i * rows, rows)], held_ref.at[i], in_sem.at[i]))
         stores.append(pltpu.make_async_copy(held_ref.at[i], out_ref.at[pl.ds(to, rows)], out_sem.at[i]))
     for load in loads:
         load.start()
@@ -401,28 +414,30 @@
     return 3.0 * square - 2.0 * cube
 
 
-def dense_half(upper, pattern, *rest):
-    return lax.dynamic_slice_in_dim(dense(upper, pattern), lax.axis_index("depth") * MR, MR, 0)
+def dense_halves(upper, pattern, *rest):
+    whole = dense(upper, pattern)
+    return whole, lax.dynamic_slice_in_dim(whole, lax.axis_index("depth") * MR, MR, 0)
 
 
 def local(upper, pattern):
     stored, slot, first, last, fits = layout(pattern)
     blocks = gather(upper, pattern, first, last)
     lists = lax.optimization_barrier(work_lists(stored, slot))
-    mine = lax.cond(fits, multiply, dense_half, upper, pattern, blocks, *lists)
+    whole, mine = lax.cond(fits, multiply, dense_halves, upper, pattern, blocks, *lists)
     other = lax.ppermute(mine, "depth", [(0, 1), (1, 0)])
     return pl.pallas_call(
         join_kernel,
         out_shape=jax.ShapeDtypeStruct(upper.shape, jnp.float32),
         in_specs=[SMEM, ANY, ANY],
         out_specs=ANY,
+        input_output_aliases={1: 0},
         scratch_shapes=[
-            pltpu.VMEM((8, MR // 4, COLS * BS), jnp.float32),
-            pltpu.SemaphoreType.DMA((8,)),
-            pltpu.SemaphoreType.DMA((8,)),
+            pltpu.VMEM((4, MR // 4, COLS * BS), jnp.float32),
+            pltpu.SemaphoreType.DMA((4,)),
+            pltpu.SemaphoreType.DMA((4,)),
         ],
         compiler_params=pltpu.CompilerParams(vmem_limit_bytes=16 * 1024 * 1024),
-    )(lax.axis_index("depth")[None].astype(jnp.int32), mine, other)
+    )(lax.axis_index("depth")[None].astype(jnp.int32), whole, other)
 
 
 def solution(mesh):

time: 170 us -> 169 us (level)
  no operation moved by 1% of the time
where the time goes in v1:
time: 169 us; the launch traced here: 168 us
  waiting for transfers between devices  90.2 us (53%)
  Pallas kernels  35.8 us (21%)
  between operations  18.6 us (11%)
  starting transfers between devices  12.1 us (7%)
  other arithmetic  6.95 us (4%)
  local copies, waits for them, and re-layouts  3.54 us (2%)
    all_gather x1, waiting for transfers between devices, gather(): return lax.all_gather(share, ALL, axis=0).reshape(STRIPS, 8, PER, 8, BS)  73.5 us
    pallas_call x1, Pallas kernels, multiply(): pl.pallas_call(main_kernel, out_shape=[jax.ShapeDtypeStruct((2 * MR, COLS...  28.4 us
    all_to_all x1, waiting for transfers between devices, gather(): lax.all_to_all(packed.reshape(NB, SRC * 8, BS), ('row', 'col'), 0, 0, til...  12.4 us
    all_to_all x1, starting transfers between devices, gather(): lax.all_to_all(packed.reshape(NB, SRC * 8, BS), ('row', 'col'), 0, 0, til...  12 us
    pallas_call x1, Pallas kernels, gather(): pl.pallas_call(pack_kernel, out_shape=jax.ShapeDtypeStruct((STRIPS, NCOL,...  4.68 us
    ppermute x1, waiting for transfers between devices, local(): other = lax.ppermute(mine, 'depth', [(0, 1), (1, 0)])  4.36 us
  transfers between devices with their start and end apart: 3, of which 3 were waited for; matrix products, arithmetic and copies ran while one was open for 7% of the time, Pallas kernels for 0%

profile of v1, /device:TPU:1, one launch (start us, length us, event | category | flops | bytes accessed | tf_op | source)
XLA Modules:
  0.0 168.3 jit_solution(18188332883406649729)
XLA Ops:
  6.6 4.7 %shard_map.37 = f32[16,4,3,8,128]{4,3,2,1,0:T(8,128)} custom-call(s32[3]{0:T(128)S(1)} %pad_add_fusion.1.here_ref, s32[64,64]{1,0:T(8,128)} %pattern_vec.1, s32[64,64]{1,0:T(8,128)} %pattern_vec.1, f32[64,8,2048]{2,1,0:T(8,128)} %bitcast.98), custom_call_target="tpu_custom_call" | custom-call | tf_op jit(solution)/shard_map/pallas_call | solution.py:261
  11.3 12.0 %all-to-all-start.2 = ((f32[64,24,128]{2,1,0:T(8,128)}), f32[64,24,128]{2,1,0:T(8,128)S(1)}, u32[]{:S(2)}, u32[]{:S(2)}) async-start(f32[64,24,128]{2,1,0:T(8,128)} %bitcast.24), calls=%async_computation.2 | async-start | bytes 1572864 | tf_op jit(solution)/shard_map/all_to_all | solution.py:269
  23.6 1.2 bitcast_reduce_fusion
  25.0 0.2 convert_reduce_fusion.3
  25.2 0.2 select_reduce_fusion.6
  25.4 12.4 %all-to-all-done.2 = f32[64,24,128]{2,1,0:T(8,128)S(1)} async-done(((f32[64,24,128]{2,1,0:T(8,128)}), f32[64,24,128]{2,1,0:T(8,128)S(1)}, u32[]{:S(2)}, u32[]{:S(2)}) %all-to-all-start.2) | async-done | bytes 786464 | tf_op jit(solution)/shard_map/all_to_all | solution.py:269
  37.8 1.2 shard_map.38
  39.1 0.5 slice.19
  40.2 0.6 slice.22
  41.0 0.2 reshape.214
  41.5 0.1 fusion.2
  41.8 2.3 %select_reduce_fusion = (s32[64,64]{1,0:T(8,128)S(1)}, s32[64,64]{1,0:T(8,128)S(1)}) fusion(s32[64,64]{1,0:T(8,128)S(1)} %fusion.2, s32[64,64]{1,0:T(8,128)S(1)} %get-tuple-element.130, s32[64,64]{1,0:T(8,128)S(1)} %fusion.4), kind=kLoop, calls=%fused_computation.20 | loop fusion | flops 1564672 | bytes 81920 | tf_op jit(solution)/shard_map/reduce_sum | solution.py:224
  44.2 0.7 select_reduce_fusion.7
  48.7 0.2 slice_reduce_fusion
  48.9 0.6 slice.23
  50.0 0.6 compare_reduce_fusion
  51.9 0.6 select_reduce_fusion.2
  52.6 0.7 concatenate.3
  53.3 0.1 convert_reduce_fusion
  53.6 73.5 %all-gather.12.cloned.1.call-done = f32[5632,8,128]{2,1,0:T(8,128)} async-done(((f32[44,8,128]{2,1,0:T(8,128)}), f32[5632,8,128]{2,1,0:T(8,128)}) %all-gather.12.cloned.1.call-update) | async-done | bytes 23068688 | tf_op jit(solution)/shard_map/all_gather | solution.py:281
  127.1 28.4 %conditional.1 = ((f32[512,2048]{1,0:T(8,128)}, f32[256,2048]{1,0:T(8,128)})) conditional(s32[]{:T(128)} %convert_element_type.91, (f32[512,2048]{1,0:T(8,128)}, s32[64,64]{1,0:T(8,128)S(1)}) %tuple.63, (f32[128,44,8,128]{3,2,1,0:T(8,128)}, s32[65,64]{1,0:T(8,128)S(1)}, s32[65,64]{1,0:T(8,128)S(1)}, s32[17,64]{1,0:T(8,128)S(1)}, ...), branch_computations={%region_21.24_spmd, %region_24.25_spmd} | conditional | flops 103089700864 | bytes 531057856 | solution.py:426
  127.1 28.4 %branch_1_fun.1 = (f32[512,2048]{1,0:T(8,128)}, f32[256,2048]{1,0:T(8,128)}) custom-call(s32[65,64]{1,0:T(8,128)S(1)} %get-tuple-element.32.sd_ref, s32[65,64]{1,0:T(8,128)S(1)} %get-tuple-element.33.st_ref, s32[17,64]{1,0:T(8,128)S(1)} %get-tuple-element.34.pd_ref, s32[17,64]{1,0:T(8,128)S(1)} %get-tuple-element.35.pt_ref, ...), custom_call_target="tpu_custom_call" | custom-call | tf_op jit(solution)/shard_map/cond/branch_1_fun/pallas_call | solution.py:310
  155.5 4.4 %collective-permute-done.other_ref = f32[256,2048]{1,0:T(8,128)S(1)} collective-permute-done((f32[256,2048]{1,0:T(8,128)}, f32[256,2048]{1,0:T(8,128)S(1)}, u32[]{:S(2)}, u32[]{:S(2)}) %collective-permute-start) | collective-permute-done | bytes 2097184 | tf_op jit(solution)/shard_map/ppermute | solution.py:427
  159.9 1.5 shard_map.39
  (57 shorter events, 2.8 us)
Async XLA Ops:
  6.5 16.8 %copy-start.1 = (s32[64,64]{1,0:T(8,128)S(1)}, s32[64,64]{1,0:T(8,128)}, u32[]{:S(2)}) copy-start(s32[64,64]{1,0:T(8,128)} %pattern_vec.1) | copy-start | bytes 49156
  6.6 46.9 %copy-start.2 = (s32[4]{0:T(128)S(1)}, s32[4]{0:T(128)}, u32[]{:S(2)}) copy-start(s32[4]{0:T(128)} %constant.149) | copy-start | bytes 52
  11.3 26.5 %all-to-all-start.2 = ((f32[64,24,128]{2,1,0:T(8,128)}), f32[64,24,128]{2,1,0:T(8,128)S(1)}, u32[]{:S(2)}, u32[]{:S(2)}) async-start(f32[64,24,128]{2,1,0:T(8,128)} %bitcast.24), calls=%async_computation.2 | async-start | bytes 1572864 | tf_op jit(solution)/shard_map/all_to_all | solution.py:269
  23.3 103.8 %all-gather.12.cloned.1.call-start = ((), (), s32[]{:S(2)}) async-start(), calls=%async_computation.8 | async-start | bytes 23248896 | tf_op jit(solution)/shard_map/all_gather | solution.py:281
  155.4 4.5 %collective-permute-start = (f32[256,2048]{1,0:T(8,128)}, f32[256,2048]{1,0:T(8,128)S(1)}, u32[]{:S(2)}, u32[]{:S(2)}) collective-permute-start(f32[256,2048]{1,0:T(8,128)} %get-tuple-element.63), channel_id=1, source_target_pairs={{0,1},{1,0},{2,3},{3,2},{4,5},{5,4},{6,7},{7,6},{8,9},{9,8},{10,11... | collective-permute-start | bytes 6291464 | tf_op jit(solution)/shard_map/ppermute | solution.py:427
Sparse Core Ops, SparseCore 0:
  39.2 87.8 all-gather.11

commit v2 on v1

--- a/solution.py
+++ b/solution.py
@@ -20,7 +20,7 @@
 SRC = 3
 HALF = 2
 MR = HALF * BS
-UNROLL = 12
+UNROLL = 16
 VMEM = 62 * 1024 * 1024
 ALL = ("row", "col", "depth")
 
@@ -132,6 +132,15 @@
     for load in loads:
         load.start()
     a_ref[...] = jnp.zeros_like(a_ref)
+
+    def clear(i, _):
+        sum_ref[i] = jnp.zeros((MR // 8, 8, BS), jnp.float32)
+        return 0
+
+    used = [(rn_ref[h] + 1) >> 1 for h in range(HALF)]
+    for h in range(HALF):
+        lax.fori_loop(h * NB // 2 + used[h], (h + 1) * NB // 2, clear, 0)
+    clear(NB, 0)
     cube_ref[...] = jnp.zeros_like(cube_ref)
     s_ref[NB] = jnp.zeros((2 * MR, BS), jnp.bfloat16)
 
@@ -162,7 +171,8 @@
             return 0
 
         lax.fori_loop(0, rn_ref[h], fill, 0)
-    sum_ref[...] = jnp.zeros_like(sum_ref)
+    for h in range(HALF):
+        lax.fori_loop(h * NB // 2, h * NB // 2 + used[h], clear, 0)
 
     def product(left_ref, list_ref, mirrored, k, p):
         c0, c1 = list_ref[k, p], list_ref[k, p + 1]

time: 169 us -> 171 us (1.012); the launches traced: 168 us -> 168 us
    pallas_call x1, Pallas kernels: 28.4 us -> 26.6 us  [multiply(): pl.pallas_call(main_kernel, out_shape=[jax.ShapeDtypeStruct((2 * MR, COLS...]
where the time goes in v2:
time: 171 us; the launch traced here: 168 us
  waiting for transfers between devices  89.8 us (53%)
  Pallas kernels  34.1 us (20%)
  between operations  18.6 us (11%)
  starting transfers between devices  13.6 us (8%)
  other arithmetic  6.94 us (4%)
  local copies, waits for them, and re-layouts  3.54 us (2%)
    all_gather x1, waiting for transfers between devices, gather(): return lax.all_gather(share, ALL, axis=0).reshape(STRIPS, 8, PER, 8, BS)  73.5 us
    pallas_call x1, Pallas kernels, multiply(): pl.pallas_call(main_kernel, out_shape=[jax.ShapeDtypeStruct((2 * MR, COLS...  26.6 us
    all_to_all x1, waiting for transfers between devices, gather(): lax.all_to_all(packed.reshape(NB, SRC * 8, BS), ('row', 'col'), 0, 0, til...  12.3 us
    all_to_all x1, starting transfers between devices, gather(): lax.all_to_all(packed.reshape(NB, SRC * 8, BS), ('row', 'col'), 0, 0, til...  11.9 us
    pallas_call x1, Pallas kernels, gather(): pl.pallas_call(pack_kernel, out_shape=jax.ShapeDtypeStruct((STRIPS, NCOL,...  4.67 us
    ppermute x1, waiting for transfers between devices, local(): other = lax.ppermute(mine, 'depth', [(0, 1), (1, 0)])  4 us
  transfers between devices with their start and end apart: 3, of which 3 were waited for; matrix products, arithmetic and copies ran while one was open for 7% of the time, Pallas kernels for 0%

profile of v2, /device:TPU:1, one launch (start us, length us, event | category | flops | bytes accessed | tf_op | source)
XLA Modules:
  0.0 167.7 jit_solution(2932916490132633156)
XLA Ops:
  6.6 4.7 %shard_map.37 = f32[16,4,3,8,128]{4,3,2,1,0:T(8,128)} custom-call(s32[3]{0:T(128)S(1)} %pad_add_fusion.1.here_ref, s32[64,64]{1,0:T(8,128)} %pattern_vec.1, s32[64,64]{1,0:T(8,128)} %pattern_vec.1, f32[64,8,2048]{2,1,0:T(8,128)} %bitcast.98), custom_call_target="tpu_custom_call" | custom-call | tf_op jit(solution)/shard_map/pallas_call | solution.py:271
  11.3 11.9 %all-to-all-start.2 = ((f32[64,24,128]{2,1,0:T(8,128)}), f32[64,24,128]{2,1,0:T(8,128)S(1)}, u32[]{:S(2)}, u32[]{:S(2)}) async-start(f32[64,24,128]{2,1,0:T(8,128)} %bitcast.24), calls=%async_computation.2 | async-start | bytes 1572864 | tf_op jit(solution)/shard_map/all_to_all | solution.py:279
  23.6 1.2 bitcast_reduce_fusion
  25.0 0.2 convert_reduce_fusion.3
  25.2 0.2 select_reduce_fusion.6
  25.4 12.3 %all-to-all-done.2 = f32[64,24,128]{2,1,0:T(8,128)S(1)} async-done(((f32[64,24,128]{2,1,0:T(8,128)}), f32[64,24,128]{2,1,0:T(8,128)S(1)}, u32[]{:S(2)}, u32[]{:S(2)}) %all-to-all-start.2) | async-done | bytes 786464 | tf_op jit(solution)/shard_map/all_to_all | solution.py:279
  37.7 1.2 shard_map.38
  39.0 0.5 slice.19
  40.1 0.6 slice.22
  41.0 0.2 reshape.214
  41.7 2.3 %select_reduce_fusion = (s32[64,64]{1,0:T(8,128)S(1)}, s32[64,64]{1,0:T(8,128)S(1)}) fusion(s32[64,64]{1,0:T(8,128)S(1)} %fusion.2, s32[64,64]{1,0:T(8,128)S(1)} %get-tuple-element.130, s32[64,64]{1,0:T(8,128)S(1)} %fusion.4), kind=kLoop, calls=%fused_computation.20 | loop fusion | flops 1564672 | bytes 81920 | tf_op jit(solution)/shard_map/reduce_sum | solution.py:234
  44.1 0.7 select_reduce_fusion.7
  48.6 0.2 slice_reduce_fusion
  48.8 0.6 slice.23
  50.0 0.6 compare_reduce_fusion
  51.8 0.6 select_reduce_fusion.2
  52.5 0.7 concatenate.3
  53.3 0.1 convert_reduce_fusion
  53.5 73.5 %all-gather.12.cloned.1.call-done = f32[5632,8,128]{2,1,0:T(8,128)} async-done(((f32[44,8,128]{2,1,0:T(8,128)}), f32[5632,8,128]{2,1,0:T(8,128)}) %all-gather.12.cloned.1.call-update) | async-done | bytes 23068688 | tf_op jit(solution)/shard_map/all_gather | solution.py:291
  127.0 26.6 %conditional.1 = ((f32[512,2048]{1,0:T(8,128)}, f32[256,2048]{1,0:T(8,128)})) conditional(s32[]{:T(128)} %convert_element_type.91, (f32[512,2048]{1,0:T(8,128)}, s32[64,64]{1,0:T(8,128)S(1)}) %tuple.63, (f32[128,44,8,128]{3,2,1,0:T(8,128)}, s32[65,64]{1,0:T(8,128)S(1)}, s32[65,64]{1,0:T(8,128)S(1)}, s32[17,64]{1,0:T(8,128)S(1)}, ...), branch_computations={%region_21.24_spmd, %region_24.25_spmd} | conditional | flops 103089700864 | bytes 531057856 | solution.py:436
  127.0 26.6 %branch_1_fun.1 = (f32[512,2048]{1,0:T(8,128)}, f32[256,2048]{1,0:T(8,128)}) custom-call(s32[65,64]{1,0:T(8,128)S(1)} %get-tuple-element.32.sd_ref, s32[65,64]{1,0:T(8,128)S(1)} %get-tuple-element.33.st_ref, s32[17,64]{1,0:T(8,128)S(1)} %get-tuple-element.34.pd_ref, s32[17,64]{1,0:T(8,128)S(1)} %get-tuple-element.35.pt_ref, ...), custom_call_target="tpu_custom_call" | custom-call | tf_op jit(solution)/shard_map/cond/branch_1_fun/pallas_call | solution.py:320
  153.7 1.6 collective-permute-start
  155.3 4.0 %collective-permute-done.other_ref = f32[256,2048]{1,0:T(8,128)S(1)} collective-permute-done((f32[256,2048]{1,0:T(8,128)}, f32[256,2048]{1,0:T(8,128)S(1)}, u32[]{:S(2)}, u32[]{:S(2)}) %collective-permute-start) | collective-permute-done | bytes 2097184 | tf_op jit(solution)/shard_map/ppermute | solution.py:437
  159.3 1.5 shard_map.39
  (57 shorter events, 2.9 us)
Async XLA Ops:
  6.5 16.8 %copy-start.1 = (s32[64,64]{1,0:T(8,128)S(1)}, s32[64,64]{1,0:T(8,128)}, u32[]{:S(2)}) copy-start(s32[64,64]{1,0:T(8,128)} %pattern_vec.1) | copy-start | bytes 49156
  6.6 46.8 %copy-start.2 = (s32[4]{0:T(128)S(1)}, s32[4]{0:T(128)}, u32[]{:S(2)}) copy-start(s32[4]{0:T(128)} %constant.164) | copy-start | bytes 52
  11.3 26.4 %all-to-all-start.2 = ((f32[64,24,128]{2,1,0:T(8,128)}), f32[64,24,128]{2,1,0:T(8,128)S(1)}, u32[]{:S(2)}, u32[]{:S(2)}) async-start(f32[64,24,128]{2,1,0:T(8,128)} %bitcast.24), calls=%async_computation.2 | async-start | bytes 1572864 | tf_op jit(solution)/shard_map/all_to_all | solution.py:279
  23.2 103.8 %all-gather.12.cloned.1.call-start = ((), (), s32[]{:S(2)}) async-start(), calls=%async_computation.8 | async-start | bytes 23248896 | tf_op jit(solution)/shard_map/all_gather | solution.py:291
  153.7 5.6 %collective-permute-start = (f32[256,2048]{1,0:T(8,128)}, f32[256,2048]{1,0:T(8,128)S(1)}, u32[]{:S(2)}, u32[]{:S(2)}) collective-permute-start(f32[256,2048]{1,0:T(8,128)} %get-tuple-element.63), channel_id=1, source_target_pairs={{0,1},{1,0},{2,3},{3,2},{4,5},{5,4},{6,7},{7,6},{8,9},{9,8},{10,11... | collective-permute-start | bytes 6291464 | tf_op jit(solution)/shard_map/ppermute | solution.py:437
Sparse Core Ops, SparseCore 0:
  39.1 87.8 all-gather.11
